TPU v7x, 32 devices: a whole 2x2x4 slice. The times are simulated.
32 devices in a mesh: attn: 4 (over z), expert: 4 (over y, x), rep: 2 (over core).
Axes of the slice: x: 2, y: 2, z: 4, core: 2. Of those that a mesh axis runs over, the one named last changes fastest.
Arguments:
- queries: bfloat16 [32, 73728], P('attn', ('expert', 'rep')), may hold values from -120 to 120
- new_latent: bfloat16 [32, 576], P('attn'), may hold values from -6 to 6
- cache_pool: bfloat16 [2048, 576], P('attn'), may hold values from -6 to 6
- local_len: int32 [4, 4], P('attn'), may hold values from 1 to 384, 512 in all within a row
- spill_cache: bfloat16 [16, 16, 576], P('attn'), may hold values from -6 to 6
- spill_owner: int32 [16], replicated, may hold values from -1 to 15, as said below
- w_uv: bfloat16 [128, 512, 128], P(('expert', 'rep')), may hold values from -0.25 to 0.25
- w_o: bfloat16 [16384, 7168], P(('expert', 'rep'), 'attn'), may hold values from -0.046875 to 0.046875
- residual: bfloat16 [32, 7168], P(None, 'attn'), may hold values from -3 to 3
- norm_gain: float32 [7168], replicated, may hold values from 0.5 to 1.5
- route_ids: int32 [32, 4], replicated, may hold values from 0 to 15, all different within a row; in each aligned block of 16 rows (0 to 15, 16 to 31, ...) at most 5 rows name the same one
- route_scores: float32 [32, 4], replicated, may hold values from 0.05 to 1
- w_gate: bfloat16 [7168, 32768], P(None, ('attn', 'expert')), may hold values from -0.0625 to 0.0625
- w_up: bfloat16 [7168, 32768], P(None, ('attn', 'expert')), may hold values from -0.0625 to 0.0625
- w_down: bfloat16 [32768, 7168], P(('attn', 'expert')), may hold values from -0.125 to 0.125
Outputs:
- mixed: bfloat16 [32, 7168], P('rep', ('attn', 'expert'))
Inputs may be any that keep to these rules, and one draw needn't show every extreme that they name: Each row of local_len sums to 512. `spill_owner`: each entry is -1 or the number of a request that lives on another index of attn than the block's slot. The slots of one index of attn hold at most 2 blocks of the requests of any one other index, and some index holds exactly 2 for some other index in every draw. `route_ids`: the token rows fall into 2 aligned blocks of 16 rows in order (2 being the size of rep); in each block no expert is named by more than 5 rows, and in some block one is named by exactly 5.
All inputs are finite; a program needn't handle non-finite values.
Results may differ from a plain program's by a relative error of at most 0.025.
Values may be sent and summed in bfloat16 or wider, within the bound.
A program may use at most 192 MiB of HBM per device.

v0:
```python
import jax
import jax.numpy as jnp
from jax import lax
from jax.sharding import PartitionSpec as P

ROPE = 64
VH = 128
EXPERTS = 16
TOP = 4
MAXLOC = 384
CAP = 2


floor_score = -1e30
scale_out = 2.5


def expert_tables(route_ids, part_index, part_count, capacity):
    row_count = route_ids.shape[0] // part_count
    route_part = lax.dynamic_slice_in_dim(route_ids, part_index * row_count, row_count, 0)
    member = jnp.any(
        route_part[:, :, None] == jnp.arange(EXPERTS, dtype=jnp.int32)[None, None, :], axis=1
    )
    order_rank = jnp.cumsum(member.astype(jnp.int32), axis=0) - 1
    slot_ids = jnp.arange(capacity, dtype=jnp.int32)
    slot_hit = member[None, :, :] & (order_rank[None, :, :] == slot_ids[:, None, None])
    place_ids = jnp.arange(row_count, dtype=jnp.int32)
    slot_token = jnp.sum(jnp.where(slot_hit, place_ids[None, :, None], 0), axis=1)
    filled = jnp.any(slot_hit, axis=1)
    return (slot_token.T, filled.T, route_part)


def per_device(
    queries,
    new_latent,
    cache_pool,
    local_len,
    spill_cache,
    spill_owner,
    w_uv,
    w_o,
    residual,
    norm_gain,
    route_ids,
    route_scores,
    w_gate,
    w_up,
    w_down,
):
    n_attn = lax.axis_size("attn")
    n_expert = lax.axis_size("expert")
    n_rep = lax.axis_size("rep")
    attn_here = lax.axis_index("attn")
    expert_here = lax.axis_index("expert")
    rep_here = lax.axis_index("rep")
    req_count = local_len.shape[1]
    head_count = w_uv.shape[0]
    row_width = new_latent.shape[1]
    lat_width = w_uv.shape[1]
    score_scale = float(VH + ROPE) ** (-0.5)
    query_rows = queries.reshape(req_count, 2, head_count, row_width)
    lengths = local_len[0]
    starts = jnp.cumsum(lengths) - lengths
    padded = jnp.concatenate([cache_pool, jnp.zeros((MAXLOC, row_width), cache_pool.dtype)], axis=0)
    windows = jax.vmap(lambda start_one: lax.dynamic_slice_in_dim(padded, start_one, MAXLOC, 0))(
        starts
    )
    local_scores = (
        jnp.einsum("rthc,rkc->rthk", query_rows, windows, preferred_element_type=jnp.float32)
        * score_scale
    )
    inside = jnp.arange(MAXLOC)[None, :] < lengths[:, None]
    local_scores = jnp.where(inside[:, None, None, :], local_scores, floor_score)
    fresh_keys = new_latent.reshape(req_count, 2, row_width)
    fresh_scores = (
        jnp.einsum("rthc,rkc->rthk", query_rows, fresh_keys, preferred_element_type=jnp.float32)
        * score_scale
    )
    causal = jnp.arange(2)[None, :] <= jnp.arange(2)[:, None]
    fresh_scores = jnp.where(causal[None, :, None, :], fresh_scores, floor_score)
    spill_count = spill_cache.shape[0]
    directory = spill_owner.reshape(n_attn, spill_count)
    owner_dev = jnp.where(directory >= 0, directory // req_count, -1)
    earlier = jnp.arange(spill_count)[:, None] > jnp.arange(spill_count)[None, :]
    same_owner = owner_dev[:, :, None] == owner_dev[:, None, :]
    order_rank = jnp.sum(same_owner & earlier[None, :, :], axis=2)
    slot_ids = jnp.arange(CAP)
    own_row = owner_dev[attn_here]
    own_rank = order_rank[attn_here]
    pick_slot = (own_row[None, None, :] == jnp.arange(n_attn)[:, None, None]) & (
        own_rank[None, None, :] == slot_ids[None, :, None]
    )
    outgoing = jnp.einsum(
        "dks,sbc->dkbc",
        pick_slot.astype(jnp.bfloat16),
        spill_cache,
        preferred_element_type=jnp.float32,
    ).astype(jnp.bfloat16)
    incoming = lax.all_to_all(outgoing, "attn", split_axis=0, concat_axis=0, tiled=True)
    mine_slot = (owner_dev[:, None, :] == attn_here) & (
        order_rank[:, None, :] == slot_ids[None, :, None]
    )
    present = jnp.any(mine_slot, axis=2).reshape(-1)
    request = jnp.sum(
        jnp.where(mine_slot, directory[:, None, :] - attn_here * req_count, 0), axis=2
    ).reshape(-1)
    blocks = incoming.reshape(n_attn * CAP, incoming.shape[2], row_width)
    slot_query = jnp.take(query_rows, request, axis=0)
    spill_scores = (
        jnp.einsum("nthc,nbc->nthb", slot_query, blocks, preferred_element_type=jnp.float32)
        * score_scale
    )
    spill_scores = jnp.where(present[:, None, None, None], spill_scores, floor_score)
    belong = (request[None, :] == jnp.arange(req_count)[:, None]) & present[None, :]
    spill_top = jnp.max(
        jnp.where(belong[:, :, None, None], jnp.max(spill_scores, axis=3)[None], floor_score),
        axis=1,
    )
    row_top = jnp.maximum(
        jnp.maximum(jnp.max(local_scores, axis=3), jnp.max(fresh_scores, axis=3)), spill_top
    )
    local_weight = jnp.exp(local_scores - row_top[..., None])
    fresh_weight = jnp.exp(fresh_scores - row_top[..., None])
    spill_weight = jnp.exp(spill_scores - jnp.take(row_top, request, axis=0)[..., None])
    spill_weight = jnp.where(present[:, None, None, None], spill_weight, 0.0)
    belong_f = belong.astype(jnp.float32)
    denominator = jnp.sum(local_weight, axis=3) + jnp.sum(fresh_weight, axis=3)
    denominator = denominator + jnp.einsum(
        "rn,nth->rth", belong_f, jnp.sum(spill_weight, axis=3), precision=lax.Precision.HIGHEST
    )
    numerator = jnp.einsum(
        "rthk,rkc->rthc",
        local_weight.astype(jnp.bfloat16),
        windows[:, :, :lat_width],
        preferred_element_type=jnp.float32,
    )
    numerator = numerator + jnp.einsum(
        "rthk,rkc->rthc",
        fresh_weight.astype(jnp.bfloat16),
        fresh_keys[:, :, :lat_width],
        preferred_element_type=jnp.float32,
    )
    spill_numer = jnp.einsum(
        "nthb,nbc->nthc",
        spill_weight.astype(jnp.bfloat16),
        blocks[:, :, :lat_width],
        preferred_element_type=jnp.float32,
    )
    numerator = numerator + jnp.einsum(
        "rn,nthc->rthc", belong_f, spill_numer, precision=lax.Precision.HIGHEST
    )
    attended = (numerator / denominator[..., None]).astype(jnp.bfloat16)
    values = jnp.einsum(
        "rthc,hcv->rthv", attended, w_uv, preferred_element_type=jnp.float32
    ).astype(jnp.bfloat16)
    values = values.reshape(2 * req_count, head_count * w_uv.shape[2])
    partial_cols = jnp.dot(
        lax.all_gather(values, "attn", axis=0, tiled=True), w_o, preferred_element_type=jnp.float32
    )
    attn_cols = lax.psum(partial_cols.astype(jnp.bfloat16), ("expert", "rep")).astype(jnp.float32)
    hidden_cols = (residual.astype(jnp.float32) + attn_cols).astype(jnp.bfloat16)
    rows_part = route_ids.shape[0] // n_rep
    capacity = rows_part * TOP // EXPERTS * 5 // 4
    shards = n_attn * n_expert // EXPERTS
    slot_token, filled, route_part = expert_tables(route_ids, rep_here, n_rep, capacity)
    part_cols = lax.dynamic_slice_in_dim(hidden_cols, rep_here * rows_part, rows_part, 0)
    dest_expert = (jnp.arange(n_attn) * n_expert + expert_here) // shards
    send_rows = jnp.take(slot_token, dest_expert, axis=0)
    send_ok = jnp.take(filled, dest_expert, axis=0)
    outgoing_rows = jnp.where(
        send_ok[:, :, None], jnp.take(part_cols, send_rows, axis=0), jnp.zeros((), jnp.bfloat16)
    )
    outgoing_rows = outgoing_rows[:, :, None, :]
    received = lax.all_to_all(outgoing_rows, "attn", split_axis=0, concat_axis=2, tiled=True)
    item_count = received.shape[1]
    full_rows = received.reshape(item_count, -1)
    widened = full_rows.astype(jnp.float32)
    normed = (
        widened * lax.rsqrt(jnp.mean(widened * widened, axis=1, keepdims=True) + 1e-06) * norm_gain
    ).astype(jnp.bfloat16)
    gate_proj = jnp.dot(normed, w_gate, preferred_element_type=jnp.float32)
    up_proj = jnp.dot(normed, w_up, preferred_element_type=jnp.float32)
    activated = (jax.nn.silu(gate_proj) * up_proj).astype(jnp.bfloat16)
    result = jnp.dot(activated, w_down, preferred_element_type=jnp.float32)
    returned_block = lax.all_to_all(
        result.reshape(1, item_count, n_attn * n_expert, -1).astype(jnp.bfloat16),
        ("attn", "expert"),
        split_axis=2,
        concat_axis=0,
        tiled=True,
    ).astype(jnp.float32)
    returned = returned_block.reshape(n_attn * n_expert, item_count, -1)
    share_part = lax.dynamic_slice_in_dim(route_scores, rep_here * rows_part, rows_part, 0)
    share_part = share_part / jnp.sum(share_part, axis=1, keepdims=True)
    share_table = jnp.sum(
        jnp.where(
            route_part[:, :, None] == jnp.arange(EXPERTS, dtype=jnp.int32)[None, None, :],
            share_part[:, :, None],
            0.0,
        ),
        axis=1,
    )
    source_expert = jnp.arange(n_attn * n_expert) // shards
    back_rows = jnp.take(slot_token, source_expert, axis=0)
    back_ok = jnp.take(filled, source_expert, axis=0)
    weight_coef = (
        jnp.where(back_ok, share_table[back_rows, source_expert[:, None]], 0.0) * scale_out
    )
    sub_cols = returned.shape[2]
    weighted = (weight_coef[:, :, None] * returned).reshape(-1, sub_cols)
    routed = jax.ops.segment_sum(weighted, back_rows.reshape(-1), num_segments=rows_part)
    own_cols = lax.dynamic_slice_in_dim(part_cols, expert_here * sub_cols, sub_cols, 1)
    return (own_cols.astype(jnp.float32) + routed).astype(jnp.bfloat16)


def solution(mesh):
    return jax.shard_map(
        per_device,
        mesh=mesh,
        in_specs=(
            P("attn", ("expert", "rep")),
            P("attn", None),
            P("attn", None),
            P("attn", None),
            P("attn", None, None),
            P(),
            P(("expert", "rep"), None, None),
            P(("expert", "rep"), "attn"),
            P(None, "attn"),
            P(),
            P(),
            P(),
            P(None, ("attn", "expert")),
            P(None, ("attn", "expert")),
            P(("attn", "expert"), None),
        ),
        out_specs=P("rep", ("attn", "expert")),
        check_vma=False,
    )
```

profile of v0, /device:TPU:0, one launch (start us, length us, event | category | flops | bytes accessed | tf_op | source)
XLA Modules:
  0.0 184.8 jit_solution(15124089280908364365)
XLA Ops:
  6.5 0.9 reshape.561
  7.7 1.1 convolution_convert_fusion.2
  8.8 0.7 copy.99
  9.5 6.3 %all-to-all-start = ((bf16[4,2,16,576]{3,2,1,0:T(8,128)(2,1)}), bf16[4,2,16,576]{3,2,1,0:T(8,128)(2,1)}, u32[]{:S(2)}, u32[]{:S(2)}) async-start(bf16[4,2,16,576]{3,2,1,0:T(8,128)(2,1)} %copy.99), calls=%async_computation | async-start | bytes 327680 | tf_op jit(solution)/shard_map/all_to_all | solution.py:99
  16.4 0.7 reshape.662
  17.1 0.7 reshape.560
  17.9 0.8 constant_dynamic-slice_fusion.2
  21.3 1.1 reshape.559
  22.6 2.2 %copy.93 = bf16[512,576]{1,0:T(8,128)(2,1)} copy(bf16[512,576]{0,1:T(8,128)(2,1)} %param.17) | data formatting | bytes 1179648 | tf_op args[2]
  25.0 1.2 concatenate.9
  26.1 8.6 %while.1 = (s32[]{:T(128)}, bf16[896,576]{1,0:T(8,128)(2,1)S(1)}, s32[4,2]{0,1:T(2,128)S(1)}, bf16[4,384,576]{2,1,0:T(8,128)(2,1)}, s32[]{:T(128)}) while((s32[]{:T(128)}, bf16[896,576]{1,0:T(8,128)(2,1)S(1)}, s32[4,2]{0,1:T(2,128)S(1)}, bf16[4,384,576]{2,1,0:T(8,128)(2,1)}, s32[]{:T(128)}) %tuple.22), condition=%wide.while_cond, body=%wide.while_body.sunk | while | flops 2 | bytes 935001 | solution.py:65
  26.8 1.5 bitcast_dynamic-update-slice_fusion.2
  28.9 1.5 bitcast_dynamic-update-slice_fusion.2
  31.1 1.5 bitcast_dynamic-update-slice_fusion.2
  33.2 1.5 bitcast_dynamic-update-slice_fusion.2
  35.6 1.7 gather_fusion.4
  38.0 2.3 %fusion.100 = (f32[4,2,16]{2,1,0:T(2,128)S(1)}, f32[4,2,16,384]{3,2,1,0:T(8,128)S(1)}) fusion(bf16[4,2,16,576]{3,2,1,0:T(8,128)(2,1)S(1)} %reshape.559, bf16[4,384,576]{2,1,0:T(8,128)(2,1)} %get-tuple-element.12, pred[4,384]{1,0:T(4,128)(4,1)S(1)} %iota_compare_fusion.2), kind=kOutput, calls=%fused_computation.161 | convolution fusion | flops 56770432 | bytes 2115584 | tf_op jit(solution)/shard_map/rthc,rkc->rthk/dot_general | solution.py:69
  40.8 1.6 fusion.99
  43.6 1.3 fusion.46
  46.8 13.9 %all_gather.3 = bf16[32,2048]{1,0:T(8,128)(2,1)S(1)} all-gather(bf16[8,2048]{1,0:T(8,128)(2,1)S(1)} %bitcast.149), channel_id=1, replica_groups=mesh['attn'=4,'expert'=4,'rep'=2] {'attn'}, dimensions={0}, use_global_device_ids=true | all-gather | bytes 163840 | tf_op jit(solution)/shard_map/all_gather | solution.py:158
  60.7 5.1 %convolution_convert_fusion.1 = bf16[32,1792]{1,0:T(8,128)(2,1)} fusion(bf16[32,2048]{1,0:T(8,128)(2,1)S(1)} %all_gather.3, bf16[2048,1792]{1,0:T(8,128)(2,1)} %param.22), kind=kOutput, calls=%fused_computation.12 | convolution fusion | flops 234938368 | bytes 7585792 | tf_op jit(solution)/shard_map/dot_general | solution.py:157
  65.8 52.7 %all-reduce.4.cloned.1.call-done = bf16[32,1792]{1,0:T(8,128)(2,1)} async-done(((bf16[32,1792]{1,0:T(8,128)(2,1)}), bf16[32,1792]{1,0:T(8,128)(2,1)}) %all-reduce.4.cloned.1.call-update) | async-done | bytes 114704 | tf_op jit(solution)/shard_map/psum | solution.py:160
  118.5 0.9 add_convert_fusion
  120.1 0.7 select_bitcast_fusion
  120.8 4.6 %all-to-all-start.1 = ((bf16[4,5,1,1792]{3,1,2,0:T(8,128)(2,1)}), bf16[4,5,1,1792]{3,1,2,0:T(8,128)(2,1)S(1)}, u32[]{:S(2)}, u32[]{:S(2)}) async-start(bf16[4,5,1,1792]{3,1,2,0:T(8,128)(2,1)} %select_bitcast_fusion), calls=%async_computation.1 | async-start | bytes 229376 | tf_op jit(solution)/shard_map/all_to_all | solution.py:174
  125.5 6.1 %all-to-all-done.1 = bf16[4,5,1,1792]{3,1,2,0:T(8,128)(2,1)S(1)} async-done(((bf16[4,5,1,1792]{3,1,2,0:T(8,128)(2,1)}), bf16[4,5,1,1792]{3,1,2,0:T(8,128)(2,1)S(1)}, u32[]{:S(2)}, u32[]{:S(2)}) %all-to-all-start.1) | async-done | bytes 71712 | tf_op jit(solution)/shard_map/all_to_all | solution.py:174
  131.8 11.4 %fusion.97 = f32[5,2048]{1,0:T(8,128)S(1)} fusion(bf16[7168,2048]{1,0:T(8,128)(2,1)} %param.27, f32[5,7168]{1,0:T(8,128)S(1)} %bitcast.138, f32[7168]{0:T(1024)S(1)} %copy-done.3, f32[5]{0:T(128)S(1)} %add_rsqrt_fusion), kind=kOutput, calls=%fused_computation.159 | convolution fusion | flops 146908160 | bytes 29573140 | tf_op jit(solution)/shard_map/dot_general | solution.py:181
  143.2 20.3 %convolution_convert_fusion = bf16[5,7168]{1,0:T(8,128)(2,1)S(1)} fusion(bf16[2048,7168]{1,0:T(8,128)(2,1)} %param.29, bf16[7168,2048]{1,0:T(8,128)(2,1)} %param.28, f32[5,2048]{1,0:T(8,128)S(1)} %fusion.97, f32[5,7168]{1,0:T(8,128)S(1)} %bitcast.139, f32[7168]{0:T(1024)S(1)} %copy-done.3, f32[5]{0:T(128)S(1)} %add_rsqrt_fusion), kind=kOutput, calls=%fused_computation.11 | convolution fusion | flops 293806080 | bytes 59004948 | tf_op jit(solution)/shard_map/dot_general | solution.py:184
  163.7 0.7 copy.115
  164.4 3.9 %all-to-all-start.2 = ((bf16[1,5,16,448]{3,1,0,2:T(8,128)(2,1)}), bf16[1,5,16,448]{3,1,0,2:T(8,128)(2,1)S(1)}, u32[]{:S(2)}, u32[]{:S(2)}) async-start(bf16[1,5,16,448]{3,1,0,2:T(8,128)(2,1)} %copy.115), calls=%async_computation.2 | async-start | bytes 262144 | tf_op jit(solution)/shard_map/all_to_all | solution.py:185
  168.7 7.4 %all-to-all-done.2 = bf16[1,5,16,448]{3,1,0,2:T(8,128)(2,1)S(1)} async-done(((bf16[1,5,16,448]{3,1,0,2:T(8,128)(2,1)}), bf16[1,5,16,448]{3,1,0,2:T(8,128)(2,1)S(1)}, u32[]{:S(2)}, u32[]{:S(2)}) %all-to-all-start.2) | async-done | bytes 71712 | tf_op jit(solution)/shard_map/all_to_all | solution.py:185
  176.2 1.2 scatter_custom_fusion
  (112 shorter events, 13.3 us)
Async XLA Ops:
  6.5 39.8 %copy-start = (bf16[16,512,128]{2,1,0:T(8,128)(2,1)S(1)}, bf16[16,512,128]{2,1,0:T(8,128)(2,1)}, u32[]{:S(2)}) copy-start(bf16[16,512,128]{2,1,0:T(8,128)(2,1)} %param.21) | copy-start | bytes 6291460
  6.5 18.2 %copy-start.6 = (s32[1,4]{1,0:T(1,128)S(1)}, s32[1,4]{1,0:T(1,128)}, u32[]{:S(2)}) copy-start(s32[1,4]{1,0:T(1,128)} %param.18) | copy-start | bytes 52
  9.5 31.3 %all-to-all-start = ((bf16[4,2,16,576]{3,2,1,0:T(8,128)(2,1)}), bf16[4,2,16,576]{3,2,1,0:T(8,128)(2,1)}, u32[]{:S(2)}, u32[]{:S(2)}) async-start(bf16[4,2,16,576]{3,2,1,0:T(8,128)(2,1)} %copy.99), calls=%async_computation | async-start | bytes 327680 | tf_op jit(solution)/shard_map/all_to_all | solution.py:99
  15.8 102.7 %all-reduce.4.cloned.1.call-start = ((), (), s32[]{:S(2)}) async-start(), calls=%async_computation.3 | async-start | bytes 229376 | tf_op jit(solution)/shard_map/psum | solution.py:160
  26.1 9.0 %copy-start.5 = (f32[32,4]{0,1:T(4,128)S(1)}, f32[32,4]{0,1:T(4,128)}, u32[]{:S(2)}) copy-start(f32[32,4]{0,1:T(4,128)} %param.26) | copy-start | bytes 1540
  43.0 2.8 %copy-start.2 = (bf16[4,384,576]{2,1,0:T(8,128)(2,1)S(1)}, bf16[4,384,576]{2,1,0:T(8,128)(2,1)}, u32[]{:S(2)}) copy-start(bf16[4,384,576]{2,1,0:T(8,128)(2,1)} %get-tuple-element.12) | copy-start | bytes 5308420
  60.7 57.8 %copy-start.4 = (bf16[32,1792]{1,0:T(8,128)(2,1)S(1)}, bf16[32,1792]{1,0:T(8,128)(2,1)}, u32[]{:S(2)}) copy-start(bf16[32,1792]{1,0:T(8,128)(2,1)} %param.23) | copy-start | bytes 344068
  65.8 66.1 %copy-start.3 = (f32[7168]{0:T(1024)S(1)}, f32[7168]{0:T(1024)}, u32[]{:S(2)}) copy-start(f32[7168]{0:T(1024)} %param.24) | copy-start | bytes 86020
  120.8 10.8 %all-to-all-start.1 = ((bf16[4,5,1,1792]{3,1,2,0:T(8,128)(2,1)}), bf16[4,5,1,1792]{3,1,2,0:T(8,128)(2,1)S(1)}, u32[]{:S(2)}, u32[]{:S(2)}) async-start(bf16[4,5,1,1792]{3,1,2,0:T(8,128)(2,1)} %select_bitcast_fusion), calls=%async_computation.1 | async-start | bytes 229376 | tf_op jit(solution)/shard_map/all_to_all | solution.py:174
  143.2 34.7 %copy-start.1 = (bf16[16,512,128]{2,1,0:T(8,128)(2,1)S(1)}, bf16[16,512,128]{2,1,0:T(8,128)(2,1)}, u32[]{:S(2)}) copy-start(bf16[16,512,128]{2,1,0:T(8,128)(2,1)} %param.21) | copy-start | bytes 6291460
  164.4 11.7 %all-to-all-start.2 = ((bf16[1,5,16,448]{3,1,0,2:T(8,128)(2,1)}), bf16[1,5,16,448]{3,1,0,2:T(8,128)(2,1)S(1)}, u32[]{:S(2)}, u32[]{:S(2)}) async-start(bf16[1,5,16,448]{3,1,0,2:T(8,128)(2,1)} %copy.115), calls=%async_computation.2 | async-start | bytes 262144 | tf_op jit(solution)/shard_map/all_to_all | solution.py:185
Sparse Core Ops, SparseCore 0:
  65.9 52.5 all-reduce.3
where the time goes:
time: 186 us; the launch traced here: 185 us
  waiting for transfers between devices  66.3 us (36%)
  matrix products  45.3 us (24%)
  local copies, waits for them, and re-layouts  24.8 us (13%)
  starting transfers between devices  14.9 us (8%)
  blocking collectives  13.9 us (7%)
  between operations  13.8 us (7%)
  other arithmetic  5.9 us (3%)
    psum x1, waiting for transfers between devices, per_device(): lax.psum(partial_cols.astype(jnp.bfloat16), ('expert', 'rep'))  52.7 us
    dot_general x1, matrix products, per_device(): result = jnp.dot(activated, w_down, preferred_element_type=jnp.float32)  20.3 us
    all_gather x1, blocking collectives, per_device(): lax.all_gather(values, 'attn', axis=0, tiled=True)  13.9 us
    dot_general x1, matrix products, per_device(): gate_proj = jnp.dot(normed, w_gate, preferred_element_type=jnp.float32)  11.4 us
    gather x12, local copies, waits for them, and re-layouts  8.61 us
    all_to_all x1, waiting for transfers between devices, per_device(): lax.all_to_all(result.reshape(1, item_count, n_attn * n_expert, -1).astyp...  7.44 us
    all_to_all x1, starting transfers between devices, per_device(): lax.all_to_all(outgoing, 'attn', split_axis=0, concat_axis=0, tiled=True)  6.32 us
    all_to_all x1, waiting for transfers between devices, per_device(): lax.all_to_all(outgoing_rows, 'attn', split_axis=0, concat_axis=2, tiled=...  6.13 us
  transfers between devices with their start and end apart: 4, of which 3 were waited for; matrix products, arithmetic and copies ran while one was open for 14% of the time, Pallas kernels for 0%

commit v1 on v0

--- a/solution.py
+++ b/solution.py
@@ -1,6 +1,8 @@
 import jax
 import jax.numpy as jnp
 from jax import lax
+from jax.experimental import pallas as pl
+from jax.experimental.pallas import tpu as pltpu
 from jax.sharding import PartitionSpec as P
 
 ROPE = 64
@@ -213,9 +215,558 @@
     return (own_cols.astype(jnp.float32) + routed).astype(jnp.bfloat16)
 
 
+def remote(src, dst, send_sem, recv_sem, target):
+    return pltpu.make_async_remote_copy(
+        src_ref=src,
+        dst_ref=dst,
+        send_sem=send_sem,
+        recv_sem=recv_sem,
+        device_id=target,
+        device_id_type=pl.DeviceIdType.MESH,
+    )
+
+
+def dot_f32(left, right):
+    return jnp.dot(left, right, preferred_element_type=jnp.float32)
+
+
+def layer_kernel(
+    q_ref,
+    new_ref,
+    pool_ref,
+    spill_ref,
+    pool_req_ref,
+    spill_req_ref,
+    pick_ref,
+    res_ref,
+    gain_ref,
+    comb_ref,
+    comb_t_ref,
+    coef_ref,
+    uv_hbm,
+    wo_hbm,
+    gate_hbm,
+    up_hbm,
+    down_hbm,
+    out_ref,
+    uv,
+    wo,
+    gate,
+    up,
+    down,
+    spill_out,
+    spill_in,
+    value_in,
+    part_out,
+    part_in,
+    row_out,
+    row_in,
+    normed,
+    pair_own,
+    pair_out,
+    pair_in,
+    back_out,
+    back_in,
+    weight_sem,
+    spill_sem,
+    value_sem,
+    part_sem,
+    row_sem,
+    pair_row_sem,
+    pair_sem,
+    back_sem,
+):
+    n_attn = lax.axis_size("attn")
+    n_expert = lax.axis_size("expert")
+    a = lax.axis_index("attn")
+    e = lax.axis_index("expert")
+    r = lax.axis_index("rep")
+    other = 1 - r
+    me = a * n_expert + e
+    plane_me = e * 2 + r
+    n_all = n_attn * n_expert
+    n_plane = n_expert * 2
+    heads = uv.shape[0]
+    lat = uv.shape[1]
+    width = pool_ref.shape[1]
+    score_scale = float(VH + ROPE) ** (-0.5)
+    half_units = gate.shape[1]
+    width_out = res_ref.shape[1]
+    piece = width_out // (2 * n_expert)
+    f32 = jnp.float32
+    bf16 = jnp.bfloat16
+
+    copies = []
+
+    def fetch(src, dst):
+        copy = pltpu.make_async_copy(src, dst, weight_sem.at[len(copies)])
+        copy.start()
+        copies.append(copy)
+
+    fetch(uv_hbm, uv)
+    rows_o = wo.shape[0] // 2
+    for i in range(2):
+        fetch(wo_hbm.at[pl.ds(i * rows_o, rows_o)], wo.at[pl.ds(i * rows_o, rows_o)])
+    cols = pl.ds(pl.multiple_of(r * half_units, 128), half_units)
+    rows_g = gate.shape[0] // 4
+    for i in range(4):
+        span = pl.ds(i * rows_g, rows_g)
+        fetch(gate_hbm.at[span, cols], gate.at[span])
+        fetch(up_hbm.at[span, cols], up.at[span])
+    rows_d = half_units // 4
+    for i in range(4):
+        begin = pl.multiple_of(r * half_units + i * rows_d, 16)
+        fetch(down_hbm.at[pl.ds(begin, rows_d)], down.at[pl.ds(i * rows_d, rows_d)])
+
+    barrier = pltpu.get_barrier_semaphore()
+    for step in range(1, n_all):
+        dest = lax.rem(me + step, n_all)
+        pl.semaphore_signal(
+            barrier,
+            inc=1,
+            device_id=(dest // n_expert, lax.rem(dest, n_expert), r),
+            device_id_type=pl.DeviceIdType.MESH,
+        )
+    for k in range(n_expert):
+        pl.semaphore_signal(
+            barrier, inc=1, device_id=(a, k, other), device_id_type=pl.DeviceIdType.MESH
+        )
+
+    spill_rows = [spill_ref[s].astype(f32) for s in range(spill_ref.shape[0])]
+    for d in range(n_attn):
+        for k in range(CAP):
+            total = pick_ref[d * CAP + k, 0] * spill_rows[0]
+            for s in range(1, len(spill_rows)):
+                total = total + pick_ref[d * CAP + k, s] * spill_rows[s]
+            spill_out[d, k] = total.astype(bf16)
+    spill_in[a] = jnp.zeros(spill_in.shape[1:], bf16)
+    pl.semaphore_wait(barrier, n_all - 1 + n_expert)
+
+    sends = []
+    for step in range(1, n_attn):
+        dest = lax.rem(a + step, n_attn)
+        copy = remote(
+            spill_out.at[dest],
+            spill_in.at[a],
+            spill_sem.at[0, dest],
+            spill_sem.at[1, a],
+            (dest, e, r),
+        )
+        copy.start()
+        sends.append(copy)
+
+    q_all = q_ref[...].astype(f32)
+    q = jnp.concatenate([q_all[:, h * width : (h + 1) * width] for h in range(heads)], axis=0)
+    q = q.astype(bf16)
+    n_rows = q.shape[0]
+    tokens = q_ref.shape[0]
+
+    def scores(keys):
+        return (
+            lax.dot_general(q, keys, (((1,), (1,)), ((), ())), preferred_element_type=f32)
+            * score_scale
+        )
+
+    def row_token(n):
+        return lax.rem(lax.broadcasted_iota(jnp.int32, (n_rows, n), 0), tokens)
+
+    pool = pool_ref[...]
+    n_pool = pool.shape[0]
+    score_pool = jnp.where(
+        pool_req_ref[...] == row_token(n_pool) // 2, scores(pool), floor_score
+    )
+    fresh = new_ref[...]
+    token_id = row_token(fresh.shape[0])
+    key_id = lax.broadcasted_iota(jnp.int32, token_id.shape, 1)
+    fresh_ok = (key_id // 2 == token_id // 2) & (key_id <= token_id)
+    score_fresh = jnp.where(fresh_ok, scores(fresh), floor_score)
+    for step in range(1, n_attn):
+        src = lax.rem(a + step, n_attn)
+        remote(
+            spill_out.at[src], spill_in.at[src], spill_sem.at[0, src], spill_sem.at[1, src], (src, e, r)
+        ).wait_recv()
+    spilled = spill_in[...].reshape(-1, width)
+    n_spill = spilled.shape[0]
+    score_spill = jnp.where(
+        spill_req_ref[...] == row_token(n_spill) // 2, scores(spilled), floor_score
+    )
+    top = jnp.maximum(
+        jnp.maximum(
+            jnp.max(score_pool, axis=1, keepdims=True), jnp.max(score_fresh, axis=1, keepdims=True)
+        ),
+        jnp.max(score_spill, axis=1, keepdims=True),
+    )
+    weight_pool = jnp.exp(score_pool - top)
+    weight_fresh = jnp.exp(score_fresh - top)
+    weight_spill = jnp.exp(score_spill - top)
+    denominator = (
+        jnp.sum(weight_pool, axis=1, keepdims=True)
+        + jnp.sum(weight_fresh, axis=1, keepdims=True)
+        + jnp.sum(weight_spill, axis=1, keepdims=True)
+    )
+    numerator = (
+        dot_f32(weight_pool.astype(bf16), pool[:, :lat])
+        + dot_f32(weight_fresh.astype(bf16), fresh[:, :lat])
+        + dot_f32(weight_spill.astype(bf16), spilled[:, :lat])
+    )
+    attended = numerator / denominator
+    copies[0].wait()
+    half_heads = heads // 2
+    sides = []
+    for side in range(2):
+        sides.append(
+            jnp.concatenate(
+                [
+                    dot_f32(attended[h * tokens : (h + 1) * tokens].astype(bf16), uv[h])
+                    for h in range(side * half_heads, (side + 1) * half_heads)
+                ],
+                axis=1,
+            )
+        )
+    value_in[a] = jnp.concatenate(sides, axis=0).astype(bf16)
+    for step in range(1, n_attn):
+        dest = lax.rem(a + step, n_attn)
+        copy = remote(
+            value_in.at[a], value_in.at[a], value_sem.at[0, dest], value_sem.at[1, a], (dest, e, r)
+        )
+        copy.start()
+        sends.append(copy)
+
+    part_rows = res_ref.shape[0] // 2
+    res_rows = res_ref[pl.ds(pl.multiple_of(r * part_rows, 16), part_rows), :].astype(f32)
+    res_piece = jnp.zeros((2 * part_rows, piece), f32)
+    for k in range(n_expert):
+        left = res_rows[:, 2 * k * piece : (2 * k + 1) * piece]
+        right = res_rows[:, (2 * k + 1) * piece : (2 * k + 2) * piece]
+        res_piece = jnp.where(e == k, jnp.concatenate([left, right], axis=0), res_piece)
+
+    for step in range(1, n_attn):
+        src = lax.rem(a + step, n_attn)
+        remote(
+            value_in.at[src], value_in.at[src], value_sem.at[0, src], value_sem.at[1, src], (src, e, r)
+        ).wait_recv()
+    gathered = [value_in[i].astype(f32) for i in range(n_attn)]
+    low = jnp.concatenate([v[:tokens] for v in gathered], axis=0).astype(bf16)
+    high = jnp.concatenate([v[tokens:] for v in gathered], axis=0).astype(bf16)
+    copies[1].wait()
+    copies[2].wait()
+    chunk = width_out // 2
+    per_chunk = n_expert // 2
+    for c in range(2):
+        partial = dot_f32(low, wo[:rows_o, c * chunk : (c + 1) * chunk]) + dot_f32(
+            high, wo[rows_o:, c * chunk : (c + 1) * chunk]
+        )
+        for k in range(per_chunk):
+            left = partial[:, 2 * k * piece : (2 * k + 1) * piece]
+            right = partial[:, (2 * k + 1) * piece : (2 * k + 2) * piece]
+            for s in range(2):
+                dest_e = c * per_chunk + k
+                dest = dest_e * 2 + s
+                lo, hi = s * part_rows, (s + 1) * part_rows
+                part_out[dest] = jnp.concatenate([left[lo:hi], right[lo:hi]], axis=0).astype(bf16)
+
+                @pl.when(dest != plane_me)
+                def _():
+                    remote(
+                        part_out.at[dest],
+                        part_in.at[plane_me],
+                        part_sem.at[0, dest],
+                        part_sem.at[1, plane_me],
+                        (a, dest_e, s),
+                    ).start()
+
+    part_in[plane_me] = part_out[plane_me]
+    for step in range(1, n_plane):
+        src = lax.rem(plane_me + step, n_plane)
+        target = (a, src // 2, lax.rem(src, 2))
+        copy = remote(
+            part_out.at[src], part_in.at[src], part_sem.at[0, src], part_sem.at[1, src], target
+        )
+        copy.wait_recv()
+        sends.append(copy)
+    projected = part_in[0].astype(f32)
+    for k in range(1, n_plane):
+        projected = projected + part_in[k].astype(f32)
+    hidden = (res_piece + projected).astype(bf16)
+
+    packed = dot_f32(comb_t_ref[...], hidden).astype(bf16)
+    slots = row_out.shape[1]
+    for j in range(n_all):
+        row_out[j] = packed[j * slots : (j + 1) * slots]
+    for step in range(1, n_all):
+        dest = lax.rem(me + step, n_all)
+        target = (dest // n_expert, lax.rem(dest, n_expert), r)
+        copy = remote(
+            row_out.at[dest], row_in.at[r, me], row_sem.at[0, dest], row_sem.at[1, me], target
+        )
+        copy.start()
+        sends.append(copy)
+    row_in[r, me] = row_out[me]
+    for step in range(1, n_all):
+        src = lax.rem(me + step, n_all)
+        target = (src // n_expert, lax.rem(src, n_expert), r)
+        remote(
+            row_out.at[src], row_in.at[r, src], row_sem.at[0, src], row_sem.at[1, src], target
+        ).wait_recv()
+    pair_rows = remote(
+        row_in.at[r], row_in.at[r], pair_row_sem.at[0], pair_row_sem.at[1], (a, e, other)
+    )
+    pair_rows.start()
+    sends.append(pair_rows)
+    remote(
+        row_in.at[other], row_in.at[other], pair_row_sem.at[0], pair_row_sem.at[1], (a, e, other)
+    ).wait_recv()
+
+    half_slots = slots // 2
+
+    def expert_rows(k):
+        first = row_in[0, k].astype(f32)
+        second = row_in[1, k].astype(f32)
+        return (
+            jnp.concatenate([first[:half_slots], second[:half_slots]], axis=0),
+            jnp.concatenate([first[half_slots:], second[half_slots:]], axis=0),
+        )
+
+    squares = jnp.zeros((slots, piece), f32)
+    for k in range(n_all):
+        left, right = expert_rows(k)
+        squares = squares + left * left + right * right
+    mean = jnp.sum(squares, axis=1, keepdims=True) / float(2 * n_all * piece)
+    inverse = lax.rsqrt(mean + 1e-06)
+    for k in range(n_all):
+        left, right = expert_rows(k)
+        normed[2 * k] = (left * inverse * gain_ref[2 * k]).astype(bf16)
+        normed[2 * k + 1] = (right * inverse * gain_ref[2 * k + 1]).astype(bf16)
+
+    for i in range(8):
+        copies[3 + i].wait()
+
+    def gate_step(k, carry):
+        gate_sum, up_sum = carry
+        rows = normed[k]
+        span = pl.ds(pl.multiple_of(k * piece, 16), piece)
+        return (gate_sum + dot_f32(rows, gate[span, :]), up_sum + dot_f32(rows, up[span, :]))
+
+    zeros = jnp.zeros((slots, half_units), f32)
+    gate_sum, up_sum = lax.fori_loop(0, 2 * n_all, gate_step, (zeros, zeros))
+    activated = (gate_sum / (1.0 + jnp.exp(-gate_sum)) * up_sum).astype(bf16)
+    for i in range(4):
+        copies[11 + i].wait()
+
+    coef = coef_ref[...]
+    n_chunk = n_all // 2
+    span_d = 4 * piece
+
+    def down_chunk(i):
+        return lax.rem(me // 2 + 1 + i, n_chunk)
+
+    def pair_copy(c):
+        return remote(
+            pair_out.at[c], pair_in.at[c], pair_sem.at[0, c], pair_sem.at[1, c], (a, e, other)
+        )
+
+    def back_copy(dest):
+        target = (dest // n_expert, lax.rem(dest, n_expert), r)
+        return remote(
+            back_out.at[dest], back_in.at[me], back_sem.at[0, dest], back_sem.at[1, me], target
+        )
+
+    def send_back(c):
+        pair_copy(c).wait_recv()
+        both = pair_own[c] + pair_in[c]
+        for p in range(2):
+            dest = 2 * c + p
+            left = both[:, 2 * p * piece : (2 * p + 1) * piece]
+            right = both[:, (2 * p + 1) * piece : (2 * p + 2) * piece]
+            back_out[dest] = jnp.concatenate([left, right], axis=0).astype(bf16)
+
+            @pl.when(dest != me)
+            def _():
+                back_copy(dest).start()
+
+    for i in range(n_chunk):
+        c = down_chunk(i)
+        result = dot_f32(activated, down[:, pl.ds(pl.multiple_of(c * span_d, 128), span_d)]) * coef
+        upper, lower = result[:half_slots], result[half_slots:]
+        pair_own[c] = jnp.where(r == 0, upper, lower)
+        pair_out[c] = jnp.where(r == 0, lower, upper)
+        pair_copy(c).start()
+        if i > 0:
+            send_back(down_chunk(i - 1))
+    send_back(down_chunk(n_chunk - 1))
+    back_in[me] = back_out[me]
+    for step in range(1, n_all):
+        src = lax.rem(me + step, n_all)
+        target = (src // n_expert, lax.rem(src, n_expert), r)
+        copy = remote(
+            back_out.at[src], back_in.at[src], back_sem.at[0, src], back_sem.at[1, src], target
+        )
+        copy.wait_recv()
+        sends.append(copy)
+    returned = back_in[...].reshape(-1, piece)
+    routed = dot_f32(comb_ref[...], returned)
+    out_ref[...] = (hidden.astype(f32) + routed).astype(bf16)
+    for i in range(n_chunk):
+        pair_copy(i).wait_send()
+    for copy in sends:
+        copy.wait_send()
+
+
+def fused_device(
+    queries,
+    new_latent,
+    cache_pool,
+    local_len,
+    spill_cache,
+    spill_owner,
+    w_uv,
+    w_o,
+    residual,
+    norm_gain,
+    route_ids,
+    route_scores,
+    w_gate,
+    w_up,
+    w_down,
+):
+    n_attn = lax.axis_size("attn")
+    n_expert = lax.axis_size("expert")
+    n_rep = lax.axis_size("rep")
+    a = lax.axis_index("attn")
+    me = a * n_expert + lax.axis_index("expert")
+    r = lax.axis_index("rep")
+    n_all = n_attn * n_expert
+    req_count = local_len.shape[1]
+    width = new_latent.shape[1]
+    pool_rows = cache_pool.shape[0]
+    piece = w_down.shape[1] // (2 * n_all)
+    half_units = w_gate.shape[1] // n_rep
+    rows_part = route_ids.shape[0] // n_rep
+    slots = 8
+
+    place = jnp.arange(pool_rows, dtype=jnp.int32)
+    before = jnp.arange(req_count)[:, None] >= jnp.arange(req_count)[None, :]
+    ends = jnp.sum(jnp.where(before, local_len[0][None, :], 0), axis=1)
+    pool_req = jnp.sum((place[None, :] >= ends[:, None]).astype(jnp.int32), axis=0)[None, :]
+
+    spill_count = spill_cache.shape[0]
+    directory = spill_owner.reshape(n_attn, spill_count)
+    owner_dev = jnp.where(directory >= 0, directory // req_count, -1)
+    earlier = jnp.arange(spill_count)[:, None] > jnp.arange(spill_count)[None, :]
+    same_owner = owner_dev[:, :, None] == owner_dev[:, None, :]
+    order_rank = jnp.sum(same_owner & earlier[None, :, :], axis=2)
+    slot_ids = jnp.arange(CAP)
+    own = jnp.arange(n_attn)[:, None] == a
+    own_row = jnp.sum(jnp.where(own, owner_dev, 0), axis=0)
+    own_rank = jnp.sum(jnp.where(own, order_rank, 0), axis=0)
+    pick = (own_row[None, None, :] == jnp.arange(n_attn)[:, None, None]) & (
+        own_rank[None, None, :] == slot_ids[None, :, None]
+    )
+    pick = pick.astype(jnp.float32).reshape(n_attn * CAP, spill_count)
+    mine = (owner_dev[:, None, :] == a) & (order_rank[:, None, :] == slot_ids[None, :, None])
+    spill_req = (
+        jnp.sum(jnp.where(mine, directory[:, None, :] - a * req_count + 1, 0), axis=2) - 1
+    )
+    block = spill_cache.shape[1]
+    spill_req = jnp.broadcast_to(spill_req.reshape(-1, 1), (n_attn * CAP, block)).reshape(1, -1)
+
+    experts = jnp.arange(EXPERTS, dtype=jnp.int32)
+    named = route_ids[:, :, None] == experts[None, None, :]
+    member = jnp.any(named, axis=1).reshape(n_rep, rows_part, EXPERTS)
+    share = route_scores / jnp.sum(route_scores, axis=1, keepdims=True)
+    share_table = jnp.sum(jnp.where(named, share[:, :, None], 0.0), axis=1)
+    share_table = share_table.reshape(n_rep, rows_part, EXPERTS)
+    row_before = jnp.arange(rows_part)[:, None] > jnp.arange(rows_part)[None, :]
+    rank = jnp.sum(member[:, None, :, :] & row_before[None, :, :, None], axis=2)
+    chosen = member[:, :, :, None] & (rank[:, :, :, None] == jnp.arange(slots))
+    at_expert = experts == me
+    coef = jnp.sum(
+        jnp.where(
+            chosen & at_expert[None, None, :, None], share_table[:, :, :, None] * scale_out, 0.0
+        ),
+        axis=(1, 2),
+    ).reshape(n_rep * slots, 1)
+    at_rep = (jnp.arange(n_rep) == r)[:, None, None, None]
+    chosen_here = jnp.any(chosen & at_rep, axis=0)
+    two = jnp.arange(2)
+    comb = (
+        chosen_here[None, :, :, None, :]
+        & (two[:, None, None, None, None] == two[None, None, None, :, None])
+    ).astype(jnp.bfloat16)
+    comb = comb.reshape(2 * rows_part, n_all * 2 * slots)
+    gain = norm_gain.reshape(2 * n_all, 1, piece)
+
+    vmem = pl.BlockSpec(memory_space=pltpu.VMEM)
+    smem = pl.BlockSpec(memory_space=pltpu.SMEM)
+    hbm = pl.BlockSpec(memory_space=pl.ANY)
+    bf16 = jnp.bfloat16
+    n_plane = n_expert * n_rep
+    dma = pltpu.SemaphoreType.DMA
+    tokens = queries.shape[0]
+    value_width = w_uv.shape[0] * w_uv.shape[2] // 2
+    out = pl.pallas_call(
+        layer_kernel,
+        out_shape=jax.ShapeDtypeStruct((2 * rows_part, piece), bf16),
+        in_specs=[vmem] * 6 + [smem] + [vmem] * 5 + [hbm] * 5,
+        out_specs=vmem,
+        scratch_shapes=[
+            pltpu.VMEM(w_uv.shape, bf16),
+            pltpu.VMEM(w_o.shape, bf16),
+            pltpu.VMEM((w_gate.shape[0], half_units), bf16),
+            pltpu.VMEM((w_up.shape[0], half_units), bf16),
+            pltpu.VMEM((half_units, w_down.shape[1]), bf16),
+            pltpu.VMEM((n_attn, CAP, block, width), bf16),
+            pltpu.VMEM((n_attn, CAP, block, width), bf16),
+            pltpu.VMEM((n_attn, 2 * tokens, value_width), bf16),
+            pltpu.VMEM((n_plane, 2 * rows_part, piece), bf16),
+            pltpu.VMEM((n_plane, 2 * rows_part, piece), bf16),
+            pltpu.VMEM((n_all, 2 * slots, piece), bf16),
+            pltpu.VMEM((n_rep, n_all, 2 * slots, piece), bf16),
+            pltpu.VMEM((2 * n_all, 2 * slots, piece), bf16),
+            pltpu.VMEM((n_all // 2, slots, 4 * piece), jnp.float32),
+            pltpu.VMEM((n_all // 2, slots, 4 * piece), jnp.float32),
+            pltpu.VMEM((n_all // 2, slots, 4 * piece), jnp.float32),
+            pltpu.VMEM((n_all, 2 * slots, piece), bf16),
+            pltpu.VMEM((n_all, 2 * slots, piece), bf16),
+            dma((15,)),
+            dma((2, n_attn)),
+            dma((2, n_attn)),
+            dma((2, n_plane)),
+            dma((2, n_all)),
+            dma((2,)),
+            dma((2, n_all // 2)),
+            dma((2, n_all)),
+        ],
+        compiler_params=pltpu.CompilerParams(
+            collective_id=0, has_side_effects=True, vmem_limit_bytes=60 * 1024 * 1024
+        ),
+    )(
+        queries,
+        new_latent,
+        cache_pool,
+        spill_cache,
+        pool_req,
+        spill_req,
+        pick,
+        residual,
+        gain,
+        comb,
+        comb.T,
+        coef,
+        w_uv,
+        w_o,
+        w_gate,
+        w_up,
+        w_down,
+    )
+    return jnp.concatenate([out[:rows_part], out[rows_part:]], axis=1)
+
+
 def solution(mesh):
+    n_attn, n_expert, n_rep = (mesh.shape[name] for name in ("attn", "expert", "rep"))
+    fused = n_attn * n_expert == EXPERTS and n_attn == 4 and n_rep == 2
     return jax.shard_map(
-        per_device,
+        fused_device if fused else per_device,
         mesh=mesh,
         in_specs=(
             P("attn", ("expert", "rep")),

time: 186 us -> 63.3 us (0.34)
  waiting for transfers between devices: 66.3 us -> 0 us
  Pallas kernels: 0 us -> 48.6 us
  matrix products: 45.3 us -> 0 us
  local copies, waits for them, and re-layouts: 24.8 us -> 7.67 us
  starting transfers between devices: 14.9 us -> 0 us
  blocking collectives: 13.9 us -> 0 us
  between operations: 13.8 us -> 0.09 us
    psum x1 -> x0, waiting for transfers between devices: 52.7 us -> none  [per_device(): lax.psum(partial_cols.astype(jnp.bfloat16), ('expert', 'rep'))]
    pallas_call x0 -> x1, Pallas kernels: none -> 48.6 us  [fused_device(): pl.pallas_call(layer_kernel, out_shape=jax.ShapeDtypeStruct((2 * rows_par...]
    dot_general x13 -> x0, matrix products: 45.3 us -> none  [the longest x1 20.3 us: per_device(): result = jnp.dot(activated, w_down, preferred_element_type=jnp.float32)]
    all_to_all x3 -> x0, starting transfers between devices: 14.8 us -> none  [the longest x1 6.32 us: per_device(): lax.all_to_all(outgoing, 'attn', split_axis=0, concat_axis=0, tiled=True)]
    gather x23 -> x0, local copies, waits for them, and re-layouts: 14.5 us -> none
    all_gather x1 -> x0, blocking collectives: 13.9 us -> none  [per_device(): lax.all_gather(values, 'attn', axis=0, tiled=True)]
    all_to_all x3 -> x0, waiting for transfers between devices: 13.6 us -> none  [the longest x1 7.44 us: per_device(): lax.all_to_all(result.reshape(1, item_count, n_attn * n_expert, -1).astyp...]
    reduce_sum x9, other arithmetic: 1.07 us -> 3.56 us  [the longest x1 0.77 us: fused_device(): ends = jnp.sum(jnp.where(before, local_len[0][None, :], 0), axis=1)]
  transfers between devices with their start and end apart: 4 -> 0, of which waited for: 3 -> 0; matrix products, arithmetic and copies ran while one was open for 14% -> 0% of each run, Pallas kernels for 0% -> 0%
where the time goes in v1:
time: 63.3 us; the launch traced here: 62.9 us
  Pallas kernels  48.6 us (77%)
  local copies, waits for them, and re-layouts  7.67 us (12%)
  other arithmetic  6.57 us (10%)
    pallas_call x1, Pallas kernels, fused_device(): pl.pallas_call(layer_kernel, out_shape=jax.ShapeDtypeStruct((2 * rows_par...  48.6 us
    unnamed x3, local copies, waits for them, and re-layouts  2.14 us
    reshape x1, local copies, waits for them, and re-layouts, fused_device(): gain = norm_gain.reshape(2 * n_all, 1, piece)  1.45 us

profile of v1, /device:TPU:0, one launch (start us, length us, event | category | flops | bytes accessed | tf_op | source)
XLA Modules:
  0.0 62.9 jit_solution(15850121935045639677)
XLA Ops:
  0.0 0.8 %select_reduce_fusion.5 = s32[4]{0:T(128)S(1)} fusion(s32[4]{0:T(128)} %bitcast.15), kind=kLoop, calls=%fused_computation.33 | loop fusion | flops 44 | bytes 32 | tf_op jit(solution)/shard_map/reduce_sum | solution.py:649
  0.8 0.7 %reduce_sum.97 = f32[32]{0:T(128)S(1)} reduce(f32[32,4]{0,1:T(4,128)} %param.26, f32[]{:T(128)} %constant.38.clone.1), dimensions={1}, to_apply=%region_9.10 | reduce | flops 96 | bytes 644 | tf_op jit(solution)/shard_map/reduce_sum | solution.py:676
  1.5 0.7 %broadcast_divide_fusion = f32[32,4]{0,1:T(4,128)S(1)} fusion(f32[32,4]{0,1:T(4,128)} %param.26, f32[32]{0:T(128)S(1)} %reduce_sum.97), kind=kLoop, calls=%fused_computation.36 | loop fusion | flops 128 | bytes 1152 | tf_op jit(solution)/shard_map/div | solution.py:676
  2.2 0.7 %convert_reduce_fusion.2 = s32[512]{0:T(512)} fusion(s32[4]{0:T(128)S(1)} %select_reduce_fusion.5), kind=kLoop, calls=%fused_computation.14 | loop fusion | flops 5632 | bytes 2064 | tf_op jit(solution)/shard_map/reduce_sum | solution.py:650
  2.9 0.7 %reshape.234 = s32[4,4]{1,0:T(4,128)S(1)} reshape(s32[16]{0:T(128)} %param.20) | data formatting | bytes 128 | tf_op jit(solution)/shard_map/reshape | solution.py:653
  3.6 0.2 convert_reduce_fusion.1
  3.8 0.2 select_reduce_fusion.2
  4.0 0.1 select_reduce_fusion.4
  4.1 0.1 copy.34
  4.2 0.1 sub.24
  4.3 0.7 %fusion.4 = pred[32,16]{0,1:T(8,128)(4,1)S(1)} fusion(s32[32,4]{0,1:T(4,128)} %param.25), kind=kLoop, calls=%fused_computation.10 | loop fusion | flops 3584 | bytes 1024 | tf_op jit(solution)/shard_map/reduce_or | solution.py:675
  5.0 0.1 copy.35
  5.1 0.6 and_convert_fusion.1
  5.7 0.1 broadcast_in_dim.76
  5.8 0.6 reshape.235.spill_req_ref
  6.4 0.7 %select_reduce_fusion.1 = f32[32,16]{0,1:T(8,128)S(1)} fusion(f32[32,4]{0,1:T(4,128)S(1)} %broadcast_divide_fusion, s32[32,4]{0,1:T(4,128)} %param.25), kind=kLoop, calls=%fused_computation.8 | loop fusion | flops 5632 | bytes 3072 | tf_op jit(solution)/shard_map/reduce_sum | solution.py:677
  7.1 0.1 copy.41
  7.2 0.1 convert_reduce_fusion
  7.3 0.1 select_reduce_fusion
  7.4 0.1 fusion.3
  7.5 0.1 copy.36
  7.6 0.7 %reshape.240.coef_ref = f32[16,1]{1,0:T(8,128)} reshape(f32[2,8]{1,0:T(2,128)S(1)} %select_reduce_fusion) | data formatting | bytes 128 | tf_op jit(solution)/shard_map/reshape | solution.py:688
  8.3 1.5 %reshape.236.gain_ref = f32[32,1,224]{2,1,0:T(1,128)} reshape(f32[7168]{0:T(1024)} %param.24) | data formatting | bytes 57344 | tf_op jit(solution)/shard_map/reshape | solution.py:697
  9.8 0.2 and_convert_fusion
  10.0 0.1 reshape.239
  10.1 0.0 copy-start
  10.1 0.7 %copy.39.comb_ref = bf16[32,256]{1,0:T(8,128)(2,1)} copy(bf16[32,256]{0,1:T(8,128)(2,1)S(1)} %reshape.239) | data formatting | bytes 32768 | tf_op jit(solution)/shard_map/convert_element_type | solution.py:695
  10.8 2.1 %copy.38.pool_ref = bf16[512,576]{1,0:T(8,128)(2,1)} copy(bf16[512,576]{0,1:T(8,128)(2,1)} %param.17) | data formatting | bytes 1179648 | tf_op args[2]
  12.9 0.0 copy-done
  12.9 48.6 %shard_map.145 = bf16[32,224]{1,0:T(8,128)(2,1)} custom-call(bf16[8,9216]{1,0:T(8,128)(2,1)} %q_ref.1, bf16[8,576]{1,0:T(8,128)(2,1)} %new_ref.1, bf16[512,576]{1,0:T(8,128)(2,1)} %copy.38.pool_ref, bf16[4,16,576]{2,1,0:T(8,128)(2,1)} %spill_ref.1, s32[1,512]{1,0:T(1,128)} %bitcast.14, s32[1,128]{1,0:T(1,128)} %reshape.235.spill_req_ref, f32[8,4]{1,0:T(8,128)} %bitcast.13, ...), custom_call_target="tpu_custom_call" | custom-call | tf_op jit(solution)/shard_map/pallas_call | solution.py:707
  61.5 0.7 %fusion.10 = (bf16[16,224]{1,0:T(8,128)(2,1)S(1)}, bf16[16,224]{1,0:T(8,128)(2,1)S(1)}) fusion(bf16[32,224]{1,0:T(8,128)(2,1)} %shard_map.145), kind=kLoop, calls=%fused_computation.44 | loop fusion | bytes 28672 | tf_op jit(solution)/shard_map/slice | solution.py:762
  62.2 0.7 %pad_maximum_fusion = bf16[16,448]{1,0:T(8,128)(2,1)} fusion(bf16[16,224]{1,0:T(8,128)(2,1)S(1)} %get-tuple-element.10, bf16[16,224]{1,0:T(8,128)(2,1)S(1)} %get-tuple-element.9), kind=kLoop, calls=%fused_computation.11 | loop fusion | flops 28672 | bytes 28672 | tf_op jit(solution)/shard_map/concatenate | solution.py:762
  (11 shorter events, 0.1 us)
Async XLA Ops:
  10.1 2.8 %copy-start = (bf16[32,256]{0,1:T(8,128)(2,1)}, bf16[32,256]{0,1:T(8,128)(2,1)S(1)}, u32[]{:S(2)}) copy-start(bf16[32,256]{0,1:T(8,128)(2,1)S(1)} %reshape.239) | copy-start | bytes 49156

commit v2 on v1

--- a/solution.py
+++ b/solution.py
@@ -235,14 +235,12 @@
     new_ref,
     pool_ref,
     spill_ref,
-    pool_req_ref,
-    spill_req_ref,
-    pick_ref,
+    len_ref,
+    owner_ref,
     res_ref,
     gain_ref,
-    comb_ref,
-    comb_t_ref,
-    coef_ref,
+    ids_ref,
+    scores_ref,
     uv_hbm,
     wo_hbm,
     gate_hbm,
@@ -333,12 +331,20 @@
         )
 
     spill_rows = [spill_ref[s].astype(f32) for s in range(spill_ref.shape[0])]
+    n_slots = len(spill_rows)
+    req_count = len_ref.shape[1]
+    own = [owner_ref[a * n_slots + s] for s in range(n_slots)]
     for d in range(n_attn):
+        totals = [jnp.zeros(spill_rows[0].shape, f32) for k in range(CAP)]
+        count = jnp.int32(0)
+        for s in range(n_slots):
+            to_d = (own[s] >= d * req_count) & (own[s] < (d + 1) * req_count)
+            for k in range(CAP):
+                factor = jnp.where(to_d & (count == k), 1.0, 0.0)
+                totals[k] = totals[k] + factor * spill_rows[s]
+            count = count + jnp.where(to_d, 1, 0)
         for k in range(CAP):
-            total = pick_ref[d * CAP + k, 0] * spill_rows[0]
-            for s in range(1, len(spill_rows)):
-                total = total + pick_ref[d * CAP + k, s] * spill_rows[s]
-            spill_out[d, k] = total.astype(bf16)
+            spill_out[d, k] = totals[k].astype(bf16)
     spill_in[a] = jnp.zeros(spill_in.shape[1:], bf16)
     pl.semaphore_wait(barrier, n_all - 1 + n_expert)
 
@@ -372,8 +378,25 @@
 
     pool = pool_ref[...]
     n_pool = pool.shape[0]
+    place = lax.broadcasted_iota(jnp.int32, (1, n_pool), 1)
+    pool_req = jnp.zeros((1, n_pool), jnp.int32)
+    end = jnp.int32(0)
+    for k in range(req_count):
+        end = end + len_ref[0, k]
+        pool_req = pool_req + jnp.where(place >= end, 1, 0)
+    block = spill_ref.shape[1]
+    column = lax.broadcasted_iota(jnp.int32, (1, n_attn * CAP * block), 1) // block
+    spill_req = jnp.full(column.shape, -1, jnp.int32)
+    for src in range(n_attn):
+        count = jnp.int32(0)
+        for s in range(n_slots):
+            request = owner_ref[src * n_slots + s] - a * req_count
+            mine = (request >= 0) & (request < req_count)
+            slot = jnp.where(mine & (count < CAP), src * CAP + count, -1)
+            spill_req = jnp.where(column == slot, request, spill_req)
+            count = count + jnp.where(mine, 1, 0)
     score_pool = jnp.where(
-        pool_req_ref[...] == row_token(n_pool) // 2, scores(pool), floor_score
+        pool_req == row_token(n_pool) // 2, scores(pool), floor_score
     )
     fresh = new_ref[...]
     token_id = row_token(fresh.shape[0])
@@ -388,7 +411,7 @@
     spilled = spill_in[...].reshape(-1, width)
     n_spill = spilled.shape[0]
     score_spill = jnp.where(
-        spill_req_ref[...] == row_token(n_spill) // 2, scores(spilled), floor_score
+        spill_req == row_token(n_spill) // 2, scores(spilled), floor_score
     )
     top = jnp.maximum(
         jnp.maximum(
@@ -439,6 +462,60 @@
         left = res_rows[:, 2 * k * piece : (2 * k + 1) * piece]
         right = res_rows[:, (2 * k + 1) * piece : (2 * k + 2) * piece]
         res_piece = jnp.where(e == k, jnp.concatenate([left, right], axis=0), res_piece)
+
+    slots = row_out.shape[1]
+    half_slots = slots // 2
+    ids = ids_ref[...]
+    n_tok = ids.shape[0]
+    share = scores_ref[...]
+    share = share / jnp.sum(share, axis=1, keepdims=True)
+    expert_id = lax.broadcasted_iota(jnp.int32, (n_tok, n_all), 1)
+    member = jnp.zeros((n_tok, n_all), f32)
+    share_table = jnp.zeros((n_tok, n_all), f32)
+    for k in range(TOP):
+        hit = ids[:, k : k + 1] == expert_id
+        member = member + jnp.where(hit, 1.0, 0.0)
+        share_table = share_table + jnp.where(hit, share[:, k : k + 1], 0.0)
+    t0 = lax.broadcasted_iota(jnp.int32, (n_tok, n_tok), 0)
+    t1 = lax.broadcasted_iota(jnp.int32, (n_tok, n_tok), 1)
+    earlier = jnp.where((t0 > t1) & (t0 // part_rows == t1 // part_rows), 1.0, 0.0)
+    rank = dot_f32(earlier.astype(bf16), member.astype(bf16))
+    member_here = jnp.where(r == 0, member[:part_rows], member[part_rows:])
+    rank_here = jnp.where(r == 0, rank[:part_rows], rank[part_rows:])
+    n_cols = n_all * slots
+    spread = jnp.where(
+        lax.broadcasted_iota(jnp.int32, (n_all, n_cols), 1) // slots
+        == lax.broadcasted_iota(jnp.int32, (n_all, n_cols), 0),
+        1.0,
+        0.0,
+    ).astype(bf16)
+    col_id = lax.broadcasted_iota(jnp.int32, (part_rows, n_cols), 1)
+    col_slot = lax.rem(col_id, half_slots).astype(f32)
+    chosen = (dot_f32(member_here.astype(bf16), spread) > 0.5) & (
+        dot_f32(rank_here.astype(bf16), spread) == col_slot
+    )
+    col_half = lax.rem(col_id // half_slots, 2)
+    comb = jnp.concatenate(
+        [jnp.where(chosen & (col_half == half), 1.0, 0.0) for half in range(2)], axis=0
+    )
+    comb_t = comb.T.astype(bf16)
+    comb = comb.astype(bf16)
+    at_me = expert_id == me
+    my_member = jnp.sum(jnp.where(at_me, member, 0.0), axis=1, keepdims=True)
+    my_rank = jnp.sum(jnp.where(at_me, rank, 0.0), axis=1, keepdims=True)
+    my_share = jnp.sum(jnp.where(at_me, share_table, 0.0), axis=1, keepdims=True)
+    slot_col = lax.broadcasted_iota(jnp.int32, (n_tok, slots), 1)
+    token_row = lax.broadcasted_iota(jnp.int32, (n_tok, slots), 0)
+    fits = (
+        (my_member > 0.5)
+        & (my_rank == lax.rem(slot_col, half_slots).astype(f32))
+        & (token_row // part_rows == slot_col // half_slots)
+    )
+    coef_row = jnp.sum(jnp.where(fits, my_share * scale_out, 0.0), axis=0, keepdims=True)
+    diagonal = lax.broadcasted_iota(jnp.int32, (slots, slots), 0) == lax.broadcasted_iota(
+        jnp.int32, (slots, slots), 1
+    )
+    coef = jnp.sum(jnp.where(diagonal, coef_row, 0.0), axis=1, keepdims=True)
 
     for step in range(1, n_attn):
         src = lax.rem(a + step, n_attn)
@@ -489,8 +566,7 @@
         projected = projected + part_in[k].astype(f32)
     hidden = (res_piece + projected).astype(bf16)
 
-    packed = dot_f32(comb_t_ref[...], hidden).astype(bf16)
-    slots = row_out.shape[1]
+    packed = dot_f32(comb_t, hidden).astype(bf16)
     for j in range(n_all):
         row_out[j] = packed[j * slots : (j + 1) * slots]
     for step in range(1, n_all):
@@ -517,8 +593,6 @@
         row_in.at[other], row_in.at[other], pair_row_sem.at[0], pair_row_sem.at[1], (a, e, other)
     ).wait_recv()
 
-    half_slots = slots // 2
-
     def expert_rows(k):
         first = row_in[0, k].astype(f32)
         second = row_in[1, k].astype(f32)
@@ -553,7 +627,6 @@
     for i in range(4):
         copies[11 + i].wait()
 
-    coef = coef_ref[...]
     n_chunk = n_all // 2
     span_d = 4 * piece
 
@@ -604,7 +677,7 @@
         copy.wait_recv()
         sends.append(copy)
     returned = back_in[...].reshape(-1, piece)
-    routed = dot_f32(comb_ref[...], returned)
+    routed = dot_f32(comb, returned)
     out_ref[...] = (hidden.astype(f32) + routed).astype(bf16)
     for i in range(n_chunk):
         pair_copy(i).wait_send()
@@ -632,68 +705,14 @@
     n_attn = lax.axis_size("attn")
     n_expert = lax.axis_size("expert")
     n_rep = lax.axis_size("rep")
-    a = lax.axis_index("attn")
-    me = a * n_expert + lax.axis_index("expert")
-    r = lax.axis_index("rep")
     n_all = n_attn * n_expert
-    req_count = local_len.shape[1]
     width = new_latent.shape[1]
-    pool_rows = cache_pool.shape[0]
     piece = w_down.shape[1] // (2 * n_all)
     half_units = w_gate.shape[1] // n_rep
     rows_part = route_ids.shape[0] // n_rep
     slots = 8
 
-    place = jnp.arange(pool_rows, dtype=jnp.int32)
-    before = jnp.arange(req_count)[:, None] >= jnp.arange(req_count)[None, :]
-    ends = jnp.sum(jnp.where(before, local_len[0][None, :], 0), axis=1)
-    pool_req = jnp.sum((place[None, :] >= ends[:, None]).astype(jnp.int32), axis=0)[None, :]
-
-    spill_count = spill_cache.shape[0]
-    directory = spill_owner.reshape(n_attn, spill_count)
-    owner_dev = jnp.where(directory >= 0, directory // req_count, -1)
-    earlier = jnp.arange(spill_count)[:, None] > jnp.arange(spill_count)[None, :]
-    same_owner = owner_dev[:, :, None] == owner_dev[:, None, :]
-    order_rank = jnp.sum(same_owner & earlier[None, :, :], axis=2)
-    slot_ids = jnp.arange(CAP)
-    own = jnp.arange(n_attn)[:, None] == a
-    own_row = jnp.sum(jnp.where(own, owner_dev, 0), axis=0)
-    own_rank = jnp.sum(jnp.where(own, order_rank, 0), axis=0)
-    pick = (own_row[None, None, :] == jnp.arange(n_attn)[:, None, None]) & (
-        own_rank[None, None, :] == slot_ids[None, :, None]
-    )
-    pick = pick.astype(jnp.float32).reshape(n_attn * CAP, spill_count)
-    mine = (owner_dev[:, None, :] == a) & (order_rank[:, None, :] == slot_ids[None, :, None])
-    spill_req = (
-        jnp.sum(jnp.where(mine, directory[:, None, :] - a * req_count + 1, 0), axis=2) - 1
-    )
     block = spill_cache.shape[1]
-    spill_req = jnp.broadcast_to(spill_req.reshape(-1, 1), (n_attn * CAP, block)).reshape(1, -1)
-
-    experts = jnp.arange(EXPERTS, dtype=jnp.int32)
-    named = route_ids[:, :, None] == experts[None, None, :]
-    member = jnp.any(named, axis=1).reshape(n_rep, rows_part, EXPERTS)
-    share = route_scores / jnp.sum(route_scores, axis=1, keepdims=True)
-    share_table = jnp.sum(jnp.where(named, share[:, :, None], 0.0), axis=1)
-    share_table = share_table.reshape(n_rep, rows_part, EXPERTS)
-    row_before = jnp.arange(rows_part)[:, None] > jnp.arange(rows_part)[None, :]
-    rank = jnp.sum(member[:, None, :, :] & row_before[None, :, :, None], axis=2)
-    chosen = member[:, :, :, None] & (rank[:, :, :, None] == jnp.arange(slots))
-    at_expert = experts == me
-    coef = jnp.sum(
-        jnp.where(
-            chosen & at_expert[None, None, :, None], share_table[:, :, :, None] * scale_out, 0.0
-        ),
-        axis=(1, 2),
-    ).reshape(n_rep * slots, 1)
-    at_rep = (jnp.arange(n_rep) == r)[:, None, None, None]
-    chosen_here = jnp.any(chosen & at_rep, axis=0)
-    two = jnp.arange(2)
-    comb = (
-        chosen_here[None, :, :, None, :]
-        & (two[:, None, None, None, None] == two[None, None, None, :, None])
-    ).astype(jnp.bfloat16)
-    comb = comb.reshape(2 * rows_part, n_all * 2 * slots)
     gain = norm_gain.reshape(2 * n_all, 1, piece)
 
     vmem = pl.BlockSpec(memory_space=pltpu.VMEM)
@@ -707,7 +726,7 @@
     out = pl.pallas_call(
         layer_kernel,
         out_shape=jax.ShapeDtypeStruct((2 * rows_part, piece), bf16),
-        in_specs=[vmem] * 6 + [smem] + [vmem] * 5 + [hbm] * 5,
+        in_specs=[vmem] * 4 + [smem] * 2 + [vmem] * 4 + [hbm] * 5,
         out_specs=vmem,
         scratch_shapes=[
             pltpu.VMEM(w_uv.shape, bf16),
@@ -745,14 +764,12 @@
         new_latent,
         cache_pool,
         spill_cache,
-        pool_req,
-        spill_req,
-        pick,
+        local_len,
+        spill_owner,
         residual,
         gain,
-        comb,
-        comb.T,
-        coef,
+        route_ids,
+        route_scores,
         w_uv,
         w_o,
         w_gate,

time: 63.3 us -> 56.7 us (0.90)
  other arithmetic: 6.57 us -> 0.68 us
    reduce_sum x9 -> x0, other arithmetic: 3.56 us -> none  [the longest x1 0.77 us: fused_device(): ends = jnp.sum(jnp.where(before, local_len[0][None, :], 0), axis=1)]
    unnamed x3, local copies, waits for them, and re-layouts: 2.14 us -> 4.88 us
    reshape x3 -> x0, local copies, waits for them, and re-layouts: 2.03 us -> none  [the longest x1 0.74 us: fused_device(): directory = spill_owner.reshape(n_attn, spill_count)]
    convert_element_type x2 -> x0, local copies, waits for them, and re-layouts: 0.8 us -> none  [fused_device(): comb = (chosen_here[None, :, :, None, :] & (two[:, None, None, None, None...]
    convert_element_type x2 -> x0, other arithmetic: 0.79 us -> none  [the longest x1 0.6 us: fused_device(): pick = pick.astype(jnp.float32).reshape(n_attn * CAP, spill_count)]
    reduce_or x2 -> x0, other arithmetic: 0.78 us -> none  [the longest x1 0.69 us: fused_device(): member = jnp.any(named, axis=1).reshape(n_rep, rows_part, EXPERTS)]
    div x1 -> x0, other arithmetic: 0.69 us -> none  [fused_device(): share = route_scores / jnp.sum(route_scores, axis=1, keepdims=True)]
where the time goes in v2:
time: 56.7 us; the launch traced here: 56.3 us
  Pallas kernels  48.6 us (86%)
  local copies, waits for them, and re-layouts  7.06 us (12%)
  other arithmetic  0.68 us (1%)
    pallas_call x1, Pallas kernels, fused_device(): pl.pallas_call(layer_kernel, out_shape=jax.ShapeDtypeStruct((2 * rows_par...  48.6 us
    unnamed x3, local copies, waits for them, and re-layouts  4.88 us
    reshape x1, local copies, waits for them, and re-layouts, fused_device(): gain = norm_gain.reshape(2 * n_all, 1, piece)  1.46 us

profile of v2, /device:TPU:0, one launch (start us, length us, event | category | flops | bytes accessed | tf_op | source)
XLA Modules:
  0.0 56.3 jit_solution(17872477627248580845)
XLA Ops:
  0.0 1.4 %copy.17.ids_ref = s32[32,4]{1,0:T(8,128)} copy(s32[32,4]{0,1:T(4,128)} %param.25) | data formatting | bytes 1024 | tf_op args[10]
  1.4 1.4 %copy.18.scores_ref = f32[32,4]{1,0:T(8,128)} copy(f32[32,4]{0,1:T(4,128)} %param.26) | data formatting | bytes 1024 | tf_op args[11]
  2.7 1.5 %reshape.3.gain_ref = f32[32,1,224]{2,1,0:T(1,128)} reshape(f32[7168]{0:T(1024)} %param.24) | data formatting | bytes 57344 | tf_op jit(solution)/shard_map/reshape | solution.py:716
  4.2 2.2 %copy.16.pool_ref = bf16[512,576]{1,0:T(8,128)(2,1)} copy(bf16[512,576]{0,1:T(8,128)(2,1)} %param.17) | data formatting | bytes 1179648 | tf_op args[2]
  6.3 48.6 %shard_map.145 = bf16[32,224]{1,0:T(8,128)(2,1)} custom-call(bf16[8,9216]{1,0:T(8,128)(2,1)} %q_ref.1, bf16[8,576]{1,0:T(8,128)(2,1)} %new_ref.1, bf16[512,576]{1,0:T(8,128)(2,1)} %copy.16.pool_ref, bf16[4,16,576]{2,1,0:T(8,128)(2,1)} %spill_ref.1, s32[1,4]{1,0:T(1,128)} %len_ref.1, s32[16]{0:T(128)} %owner_ref.1, bf16[32,1792]{1,0:T(8,128)(2,1)} %res_ref.1, ...), custom_call_target="tpu_custom_call" | custom-call | tf_op jit(solution)/shard_map/pallas_call | solution.py:726
  54.9 0.7 %fusion = (bf16[16,224]{1,0:T(8,128)(2,1)S(1)}, bf16[16,224]{1,0:T(8,128)(2,1)S(1)}) fusion(bf16[32,224]{1,0:T(8,128)(2,1)} %shard_map.145), kind=kLoop, calls=%fused_computation.1 | loop fusion | bytes 28672 | tf_op jit(solution)/shard_map/slice | solution.py:779
  55.6 0.7 %pad_maximum_fusion = bf16[16,448]{1,0:T(8,128)(2,1)} fusion(bf16[16,224]{1,0:T(8,128)(2,1)S(1)} %get-tuple-element.6, bf16[16,224]{1,0:T(8,128)(2,1)S(1)} %get-tuple-element.5), kind=kLoop, calls=%fused_computation | loop fusion | flops 28672 | bytes 28672 | tf_op jit(solution)/shard_map/concatenate | solution.py:779
